TPU v7x, 32 devices: a whole 2x2x4 slice. The times are simulated.
32 devices in a mesh: groups: 2 (over x), blk: 16 (over z, y, core).
Axes of the slice: x: 2, y: 2, z: 4, core: 2. Of those that a mesh axis runs over, the one named last changes fastest.
Arguments:
- wavefunction: bfloat16 [384, 128, 128], P(('groups', 'blk')), parts along dimension 0, may hold values from -6 to 6
- left_blocks: bfloat16 [7680, 128, 128], P(('groups', 'blk')), parts along dimension 0, may hold values from -0.5 to 0.5
- right_blocks: bfloat16 [2560, 128, 128], P(('groups', 'blk')), parts along dimension 0, may hold values from -0.078125 to 0.078125
- right_env: int32 [64, 40], P(('groups', 'blk')), parts along dimension 0, may hold values from 0 to 1279, as said below
- pair_sectors: int32 [384, 2], P(('groups', 'blk')), parts along dimension 0, may hold values from 0 to 5, as said below
- channel_mask: int32 [384, 40], P(('groups', 'blk')), parts along dimension 0, may hold values 0 or 1
Outputs:
- applied_state: float32 [384, 128, 128], P(('groups', 'blk')), parts along dimension 0
There are 2 independent parts, one for each index of `groups`. A program takes and returns all parts, laid end to end along the dimension named above; each array names one. Nothing has to cross between parts.
Inputs may be any that keep to these rules, and one draw needn't show every extreme that they name: `right_env`: the 80 entries of one device are distinct; among them no owner device (entry // 80) is named more than 8 times, and some owner exactly 8 times. Devices may name the same blocks. `pair_sectors`: on each device the pairs list every combination of a left sector index below 6 and a right sector index below 2 exactly once.
All inputs are finite; a program needn't handle non-finite values. No bound on the sum of `channel_mask` on one device may be relied on, other than what follows from the above.
Results may differ from a plain program's by a relative error of at most 0.0041.
Values may be sent and summed in bfloat16 or wider, within the bound.
A program may use at most 128 MiB of HBM per device.

v0:
```python
import jax
import jax.numpy as jnp
from jax import lax
from jax.sharding import PartitionSpec as P


def slot_ranks(owners, peers):
    onehot = (owners[:, None] == jnp.arange(peers, dtype=jnp.int32)[None, :]).astype(jnp.int32)
    return jnp.sum(jnp.cumsum(onehot, axis=0) * onehot, axis=1) - 1


def on_device(wavefunction, left_blocks, right_blocks, right_env, pair_sectors, channel_mask):
    pairs = wavefunction.shape[0]
    tile = wavefunction.shape[1]
    channels = channel_mask.shape[1]
    sectors = right_env.shape[0]
    lefts = left_blocks.reshape(left_blocks.shape[0] // channels, channels, tile, tile)
    stored = right_blocks.shape[0]
    peers = lax.axis_size("blk")
    used = sectors * channels
    capacity = max(2, (3 * used + 2 * peers - 1) // (2 * peers))
    slots = lefts.shape[0] * capacity
    wanted = right_env[pair_sectors[:, 1]].reshape(pairs * channels)
    owners = wanted // stored
    position = owners * slots + slot_ranks(owners, peers)
    requests = jnp.zeros((peers * slots,), jnp.int32).at[position].set(wanted % stored)
    asked = lax.all_to_all(
        requests.reshape(peers, slots), "blk", split_axis=0, concat_axis=0, tiled=True
    )
    replies = right_blocks[asked.reshape(peers * slots)].reshape(peers, slots, tile, tile)
    fetched = lax.all_to_all(replies, "blk", split_axis=0, concat_axis=0, tiled=True)
    places = position.reshape(pairs, channels)
    received = fetched.reshape(peers * slots, tile, tile)
    weights = channel_mask.astype(jnp.bfloat16)

    def one_pair(index):
        left = lefts[pair_sectors[index, 0]]
        state = wavefunction[index]
        lifted = jnp.einsum("aij,jk->aik", left, state, preferred_element_type=jnp.float32).astype(
            jnp.bfloat16
        )
        right = received[places[index]]
        applied = jnp.einsum(
            "aik,amk->aim", lifted, right, preferred_element_type=jnp.float32
        ).astype(jnp.bfloat16)
        return jnp.einsum("a,aim->im", weights[index], applied, preferred_element_type=jnp.float32)

    return lax.map(one_pair, jnp.arange(pairs, dtype=jnp.int32))


def solution(mesh):
    placed = (
        P(("groups", "blk"), None, None),
        P(("groups", "blk"), None, None),
        P(("groups", "blk"), None, None),
        P(("groups", "blk"), None),
        P(("groups", "blk"), None),
        P(("groups", "blk"), None),
    )
    return jax.shard_map(
        on_device,
        mesh=mesh,
        in_specs=placed,
        out_specs=P(("groups", "blk"), None, None),
        check_vma=False,
    )
```

profile of v0, /device:TPU:9, one launch (start us, length us, event | category | flops | bytes accessed | tf_op | source)
XLA Modules:
  0.0 851.2 jit_solution(10560190351316254387)
XLA Ops:
  0.0 0.8 fusion.24
  0.8 1.2 gather_fusion.1
  2.5 1.2 reduce-window.6
  4.3 2.9 scatter_custom_fusion
  7.3 11.1 %all_to_all.14 = s32[16,1,48]{2,1,0:T(1,128)S(1)} all-to-all(s32[16,1,48]{2,1,0:T(1,128)S(1)} %all_to_all.9), channel_id=1, replica_groups=mesh['groups'=2,'blk'=16] {'blk'}, dimensions={0} | all-to-all | bytes 6144 | tf_op jit(solution)/shard_map/all_to_all | solution.py:27
  18.9 0.7 reduce.7
  19.7 19.0 %gather_fusion.2 = bf16[768,128,128]{2,1,0:T(8,128)(2,1)} fusion(bf16[80,128,128]{2,1,0:T(8,128)(2,1)S(1)} %copy-done, s32[1024]{0:T(1024)S(1)} %pad_clamp_fusion.1), kind=kCustom, calls=%fused_computation.2 | custom fusion | bytes 50334720 | tf_op jit(solution)/shard_map/gather | solution.py:30
  38.7 7.2 all-to-all-start.1
  45.9 539.7 %all-to-all-done.1 = bf16[16,48,128,128]{3,2,1,0:T(8,128)(2,1)} async-done(((bf16[16,48,128,128]{3,2,1,0:T(8,128)(2,1)}), bf16[16,48,128,128]{3,2,1,0:T(8,128)(2,1)}, u32[]{:S(2)}, u32[]{:S(2)}) %all-to-all-start.1) | async-done | bytes 25165856 | tf_op jit(solution)/shard_map/all_to_all | solution.py:31
  585.6 265.6 %while.10 = (s32[]{:T(128)}, f32[12,128,128]{2,1,0:T(8,128)}, s32[12]{0:T(128)S(1)}, bf16[12,40]{1,0:T(8,128)(2,1)S(1)}, s32[12,2]{0,1:T(2,128)S(1)}, /*index=5*...) while((s32[]{:T(128)}, f32[12,128,128]{2,1,0:T(8,128)}, ...), condition=%wide.region_5.6_spmd, body=%wide.region_4.5_spmd.sunk | while | flops 338166912 | bytes 8099689 | solution.py:48
  590.6 10.1 %gather_fusion = bf16[40,128,128]{2,1,0:T(8,128)(2,1)} fusion(bf16[768,128,128]{2,1,0:T(8,128)(2,1)} %get-tuple-element.166, s32[1024]{0:T(1024)S(1)} %pad_clamp_fusion.4), kind=kCustom, calls=%fused_computation.clone.1 | custom fusion | bytes 2621600 | tf_op jit(solution)/shard_map/while/body/eval_jaxpr/gather | solution.py:42
  600.7 4.2 convolution_convert_fusion.3
  604.9 2.2 fusion.39
  607.1 0.6 constant_dynamic-update-slice_fusion.2
  612.7 10.1 %gather_fusion = bf16[40,128,128]{2,1,0:T(8,128)(2,1)} fusion(bf16[768,128,128]{2,1,0:T(8,128)(2,1)} %get-tuple-element.166, s32[1024]{0:T(1024)S(1)} %pad_clamp_fusion.4), kind=kCustom, calls=%fused_computation.clone.1 | custom fusion | bytes 2621600 | tf_op jit(solution)/shard_map/while/body/eval_jaxpr/gather | solution.py:42
  622.9 4.2 convolution_convert_fusion.3
  627.0 2.2 fusion.39
  634.9 10.1 %gather_fusion = bf16[40,128,128]{2,1,0:T(8,128)(2,1)} fusion(bf16[768,128,128]{2,1,0:T(8,128)(2,1)} %get-tuple-element.166, s32[1024]{0:T(1024)S(1)} %pad_clamp_fusion.4), kind=kCustom, calls=%fused_computation.clone.1 | custom fusion | bytes 2621600 | tf_op jit(solution)/shard_map/while/body/eval_jaxpr/gather | solution.py:42
  645.0 4.2 convolution_convert_fusion.3
  649.2 2.2 fusion.39
  651.4 0.6 constant_dynamic-update-slice_fusion.2
  657.0 10.1 %gather_fusion = bf16[40,128,128]{2,1,0:T(8,128)(2,1)} fusion(bf16[768,128,128]{2,1,0:T(8,128)(2,1)} %get-tuple-element.166, s32[1024]{0:T(1024)S(1)} %pad_clamp_fusion.4), kind=kCustom, calls=%fused_computation.clone.1 | custom fusion | bytes 2621600 | tf_op jit(solution)/shard_map/while/body/eval_jaxpr/gather | solution.py:42
  667.1 4.2 convolution_convert_fusion.3
  671.3 2.2 fusion.39
  679.1 10.1 %gather_fusion = bf16[40,128,128]{2,1,0:T(8,128)(2,1)} fusion(bf16[768,128,128]{2,1,0:T(8,128)(2,1)} %get-tuple-element.166, s32[1024]{0:T(1024)S(1)} %pad_clamp_fusion.4), kind=kCustom, calls=%fused_computation.clone.1 | custom fusion | bytes 2621600 | tf_op jit(solution)/shard_map/while/body/eval_jaxpr/gather | solution.py:42
  689.3 4.2 convolution_convert_fusion.3
  693.4 2.2 fusion.39
  701.3 10.1 %gather_fusion = bf16[40,128,128]{2,1,0:T(8,128)(2,1)} fusion(bf16[768,128,128]{2,1,0:T(8,128)(2,1)} %get-tuple-element.166, s32[1024]{0:T(1024)S(1)} %pad_clamp_fusion.4), kind=kCustom, calls=%fused_computation.clone.1 | custom fusion | bytes 2621600 | tf_op jit(solution)/shard_map/while/body/eval_jaxpr/gather | solution.py:42
  711.4 4.2 convolution_convert_fusion.3
  715.6 2.2 fusion.39
  723.4 10.1 %gather_fusion = bf16[40,128,128]{2,1,0:T(8,128)(2,1)} fusion(bf16[768,128,128]{2,1,0:T(8,128)(2,1)} %get-tuple-element.166, s32[1024]{0:T(1024)S(1)} %pad_clamp_fusion.4), kind=kCustom, calls=%fused_computation.clone.1 | custom fusion | bytes 2621600 | tf_op jit(solution)/shard_map/while/body/eval_jaxpr/gather | solution.py:42
  733.5 4.2 convolution_convert_fusion.3
  737.7 2.2 fusion.39
  745.5 10.1 %gather_fusion = bf16[40,128,128]{2,1,0:T(8,128)(2,1)} fusion(bf16[768,128,128]{2,1,0:T(8,128)(2,1)} %get-tuple-element.166, s32[1024]{0:T(1024)S(1)} %pad_clamp_fusion.4), kind=kCustom, calls=%fused_computation.clone.1 | custom fusion | bytes 2621600 | tf_op jit(solution)/shard_map/while/body/eval_jaxpr/gather | solution.py:42
  755.7 4.2 convolution_convert_fusion.3
  759.8 2.2 fusion.39
  767.7 10.1 %gather_fusion = bf16[40,128,128]{2,1,0:T(8,128)(2,1)} fusion(bf16[768,128,128]{2,1,0:T(8,128)(2,1)} %get-tuple-element.166, s32[1024]{0:T(1024)S(1)} %pad_clamp_fusion.4), kind=kCustom, calls=%fused_computation.clone.1 | custom fusion | bytes 2621600 | tf_op jit(solution)/shard_map/while/body/eval_jaxpr/gather | solution.py:42
  777.8 4.2 convolution_convert_fusion.3
  782.0 2.2 fusion.39
  789.8 10.1 %gather_fusion = bf16[40,128,128]{2,1,0:T(8,128)(2,1)} fusion(bf16[768,128,128]{2,1,0:T(8,128)(2,1)} %get-tuple-element.166, s32[1024]{0:T(1024)S(1)} %pad_clamp_fusion.4), kind=kCustom, calls=%fused_computation.clone.1 | custom fusion | bytes 2621600 | tf_op jit(solution)/shard_map/while/body/eval_jaxpr/gather | solution.py:42
  799.9 4.2 convolution_convert_fusion.3
  804.1 2.2 fusion.39
  811.9 10.1 %gather_fusion = bf16[40,128,128]{2,1,0:T(8,128)(2,1)} fusion(bf16[768,128,128]{2,1,0:T(8,128)(2,1)} %get-tuple-element.166, s32[1024]{0:T(1024)S(1)} %pad_clamp_fusion.4), kind=kCustom, calls=%fused_computation.clone.1 | custom fusion | bytes 2621600 | tf_op jit(solution)/shard_map/while/body/eval_jaxpr/gather | solution.py:42
  822.1 4.2 convolution_convert_fusion.3
  826.2 2.2 fusion.39
  834.1 10.1 %gather_fusion = bf16[40,128,128]{2,1,0:T(8,128)(2,1)} fusion(bf16[768,128,128]{2,1,0:T(8,128)(2,1)} %get-tuple-element.166, s32[1024]{0:T(1024)S(1)} %pad_clamp_fusion.4), kind=kCustom, calls=%fused_computation.clone.1 | custom fusion | bytes 2621600 | tf_op jit(solution)/shard_map/while/body/eval_jaxpr/gather | solution.py:42
  844.2 4.2 convolution_convert_fusion.3
  848.4 2.2 fusion.39
  (92 shorter events, 22.6 us)
Async XLA Ops:
  0.0 19.7 %copy-start = (bf16[80,128,128]{2,1,0:T(8,128)(2,1)S(1)}, bf16[80,128,128]{2,1,0:T(8,128)(2,1)}, u32[]{:S(2)}) copy-start(bf16[80,128,128]{2,1,0:T(8,128)(2,1)} %param.10) | copy-start | bytes 7864324
  38.7 7.2 copy-start.1
  38.7 546.9 %copy-start.2 = (s32[12,2]{0,1:T(2,128)S(1)}, s32[12,2]{0,1:T(2,128)}, u32[]{:S(2)}) copy-start(s32[12,2]{0,1:T(2,128)} %param.12) | copy-start | bytes 292
  38.7 546.9 %all-to-all-start.1 = ((bf16[16,48,128,128]{3,2,1,0:T(8,128)(2,1)}), bf16[16,48,128,128]{3,2,1,0:T(8,128)(2,1)}, u32[]{:S(2)}, u32[]{:S(2)}) async-start(bf16[16,48,128,128]{3,2,1,0:T(8,128)(2,1)} %bitcast.65), calls=%async_computation.1 | async-start | bytes 50331648 | tf_op jit(solution)/shard_map/all_to_all | solution.py:31
where the time goes:
time: 856 us; the launch traced here: 851 us
  waiting for transfers between devices  540 us (63%)
  local copies, waits for them, and re-layouts  168 us (20%)
  matrix products  76.9 us (9%)
  loops' own time  45.3 us (5%)
  blocking collectives  11.1 us (1%)
    all_to_all x1, waiting for transfers between devices, on_device(): lax.all_to_all(replies, 'blk', split_axis=0, concat_axis=0, tiled=True)  540 us
    gather x12, local copies, waits for them, and re-layouts, one_pair(): right = received[places[index]]  121 us
    dot_general x12, matrix products, one_pair(): jnp.einsum('aik,amk->aim', lifted, right, preferred_element_type=jnp.floa...  50.2 us
    another operation x1, loops' own time, on_device(): return lax.map(one_pair, jnp.arange(pairs, dtype=jnp.int32))  45.3 us
    dot_general x12, matrix products, one_pair(): jnp.einsum('a,aim->im', weights[index], applied, preferred_element_type=j...  26.7 us
    gather x1, local copies, waits for them, and re-layouts, on_device(): right_blocks[asked.reshape(peers * slots)].reshape(peers, slots, tile, tile)  19 us
  transfers between devices with their start and end apart: 1, of which 1 were waited for; matrix products, arithmetic and copies ran while one was open for 0% of the time, Pallas kernels for 0%

commit v1 on v0

v1 whole, which is shorter than its diff:
```python
import functools

import jax
import jax.numpy as jnp
from jax import lax
from jax.experimental import pallas as pl
from jax.experimental.pallas import tpu as pltpu
from jax.sharding import PartitionSpec as P

MESH = pl.DeviceIdType.MESH


def flip(index, step, n):
    out = 0
    bit = 1
    while bit < n:
        out = out + bit * ((index // bit + step // bit) % 2)
        bit *= 2
    return out


def kernel(
    n,
    cap,
    sectors_l,
    channels,
    request_ref,
    entry_ref,
    side_ref,
    place_ref,
    pairs_ref,
    mask_ref,
    psi_ref,
    left_hbm,
    right_hbm,
    out_ref,
    left,
    right,
    asked,
    asked_sc,
    send,
    held,
    lifted,
    total,
    left_sem,
    right_sem,
    ask_send_sem,
    ask_recv_sem,
    table_sem,
    send_sem,
    recv_sem,
):
    me = lax.axis_index("blk")
    tile = psi_ref.shape[1]
    pairs = psi_ref.shape[0]
    right_copy = pltpu.make_async_copy(right_hbm, right, right_sem)
    right_copy.start()

    def left_copy(l):
        return pltpu.make_async_copy(
            left_hbm.at[pl.ds(l * channels, channels)],
            left.at[pl.ds(l * channels, channels)],
            left_sem.at[l],
        )

    for l in range(sectors_l):
        left_copy(l).start()

    barrier = pltpu.get_barrier_semaphore()

    def greet(k, c):
        pl.semaphore_signal(barrier, inc=1, device_id={"blk": flip(me, k, n)}, device_id_type=MESH)
        return c

    lax.fori_loop(1, n, greet, 0)
    pl.semaphore_wait(barrier, n - 1)

    def ask(k):
        peer = flip(me, k, n)
        return pltpu.make_async_remote_copy(
            src_ref=request_ref.at[peer],
            dst_ref=asked.at[k],
            send_sem=ask_send_sem.at[k],
            recv_sem=ask_recv_sem.at[k],
            device_id={"blk": peer},
            device_id_type=MESH,
        )

    def ask_start(k, c):
        ask(n - k).start()
        return c

    lax.fori_loop(1, n, ask_start, 0)
    asked[0] = request_ref[me]

    def reply(k):
        return pltpu.make_async_remote_copy(
            src_ref=send.at[k],
            dst_ref=held.at[k],
            send_sem=send_sem.at[k],
            recv_sem=recv_sem.at[k],
            device_id={"blk": flip(me, k, n)},
            device_id_type=MESH,
        )

    def ask_wait(k, c):
        ask(n - k).wait()
        return c

    lax.fori_loop(1, n, ask_wait, 0)
    table_copy = pltpu.make_async_copy(asked, asked_sc, table_sem)
    table_copy.start()
    right_copy.wait()
    table_copy.wait()

    def pack(i, c):
        k = n - i

        for j in range(cap):
            send[k, j] = right[asked_sc[k, 0, j]]
        reply(k).start()
        return c

    lax.fori_loop(1, n, pack, 0)
    for j in range(cap):
        held[0, j] = right[asked_sc[0, 0, j]]

    def lift(l, c):
        left_copy(l).wait()
        p0 = place_ref[2 * l]
        p1 = place_ref[2 * l + 1]
        state = jnp.concatenate([psi_ref[p0], psi_ref[p1]], axis=1)

        def one(a, c):
            both = jnp.dot(left[l * channels + a], state, preferred_element_type=jnp.float32)
            m0 = mask_ref[p0, a].astype(jnp.float32)
            m1 = mask_ref[p1, a].astype(jnp.float32)
            lifted[a, l] = (both[:, :tile] * m0).astype(jnp.bfloat16)
            lifted[channels + a, l] = (both[:, tile:] * m1).astype(jnp.bfloat16)
            return c

        return lax.fori_loop(0, channels, one, c)

    lax.fori_loop(0, sectors_l, lift, 0)
    total[...] = jnp.zeros_like(total)

    def apply(k):
        peer = flip(me, k, n)

        def two(h, c):
            rows = []
            entries = []
            for j in range(2):
                s = peer * cap + 2 * h + j
                entries.append(entry_ref[s])
                block = held[k, 2 * h + j].astype(jnp.float32)
                w0 = (side_ref[s] % 2).astype(jnp.float32)
                w1 = (side_ref[s] // 2).astype(jnp.float32)
                rows.append(
                    jnp.concatenate([(block * w0).astype(jnp.bfloat16), (block * w1).astype(jnp.bfloat16)], axis=0)
                )
            wide = jnp.concatenate(rows, axis=1)

            for l in range(sectors_l):
                x = jnp.concatenate([lifted[entries[0], l], lifted[entries[1], l]], axis=1)
                total[l] += lax.dot_general(
                    x, wide, (((1,), (1,)), ((), ())), preferred_element_type=jnp.float32
                )
            return c

        lax.fori_loop(0, cap // 2, two, 0)

    apply(0)

    def arrive(i, c):
        k = n - i
        reply(k).wait_recv()
        apply(k)
        return c

    lax.fori_loop(1, n, arrive, 0)

    def finish(p, c):
        both = total[pairs_ref[2 * p]]
        w1 = pairs_ref[2 * p + 1].astype(jnp.float32)
        out_ref[p] = both[:, :tile] * (1.0 - w1) + both[:, tile:] * w1
        return c

    lax.fori_loop(0, pairs, finish, 0)

    def sent(k, c):
        reply(k).wait_send()
        return c

    lax.fori_loop(1, n, sent, 0)


def on_device(n, wavefunction, left_blocks, right_blocks, right_env, pair_sectors, channel_mask):
    pairs, tile = wavefunction.shape[0], wavefunction.shape[1]
    channels = channel_mask.shape[1]
    sides = right_env.shape[0]
    sectors_l = left_blocks.shape[0] // channels
    stored = right_blocks.shape[0]
    used = sides * channels
    cap = max(2, (3 * used + 2 * n - 1) // (2 * n))
    cap += cap % 2

    ids = right_env.reshape(used)
    owners = ids // stored
    order = jnp.arange(used, dtype=jnp.int32)
    same = (owners[:, None] == owners[None, :]) & (order[None, :] < order[:, None])
    rank = jnp.sum(same.astype(jnp.int32), axis=1)
    slot = owners * cap + rank
    chosen = slot[None, :] == jnp.arange(n * cap, dtype=jnp.int32)[:, None]
    entry = jnp.sum(jnp.where(chosen, order[None, :], 0), axis=1)
    side = jnp.sum(jnp.where(chosen, 1 + (order // channels)[None, :], 0), axis=1)
    request = jnp.sum(jnp.where(chosen, (ids % stored)[None, :], 0), axis=1)
    request = jnp.pad(request.reshape(n, 1, cap), ((0, 0), (0, 0), (0, 128 - cap)))
    spot = pair_sectors[:, 0] * sides + pair_sectors[:, 1]
    which = jnp.arange(pairs, dtype=jnp.int32)
    place = jnp.sum(jnp.where(spot[None, :] == which[:, None], which[None, :], 0), axis=1)

    smem = pl.BlockSpec(memory_space=pltpu.SMEM)
    vmem = pl.BlockSpec(memory_space=pltpu.VMEM)
    hbm = pl.BlockSpec(memory_space=pl.ANY)
    return pl.pallas_call(
        functools.partial(kernel, n, cap, sectors_l, channels),
        out_shape=jax.ShapeDtypeStruct((pairs, tile, tile), jnp.float32),
        in_specs=[vmem, smem, smem, smem, smem, smem, vmem, hbm, hbm],
        out_specs=vmem,
        scratch_shapes=[
            pltpu.VMEM(left_blocks.shape, jnp.bfloat16),
            pltpu.VMEM(right_blocks.shape, jnp.bfloat16),
            pltpu.VMEM((n, 1, 128), jnp.int32),
            pltpu.SMEM((n, 1, 128), jnp.int32),
            pltpu.VMEM((n, cap, tile, tile), jnp.bfloat16),
            pltpu.VMEM((n, cap, tile, tile), jnp.bfloat16),
            pltpu.VMEM((used, sectors_l, tile, tile), jnp.bfloat16),
            pltpu.VMEM((sectors_l, tile, 2 * tile), jnp.float32),
            pltpu.SemaphoreType.DMA((sectors_l,)),
            pltpu.SemaphoreType.DMA,
            pltpu.SemaphoreType.DMA((n,)),
            pltpu.SemaphoreType.DMA((n,)),
            pltpu.SemaphoreType.DMA,
            pltpu.SemaphoreType.DMA((n,)),
            pltpu.SemaphoreType.DMA((n,)),
        ],
        compiler_params=pltpu.CompilerParams(
            collective_id=0, has_side_effects=True, vmem_limit_bytes=56 * 1024 * 1024
        ),
    )(
        request,
        entry,
        side,
        place,
        pair_sectors.reshape(-1),
        channel_mask,
        wavefunction,
        left_blocks,
        right_blocks,
    )


def solution(mesh):
    row = P(("groups", "blk"), None)
    block = P(("groups", "blk"), None, None)
    return jax.shard_map(
        functools.partial(on_device, mesh.shape["blk"]),
        mesh=mesh,
        in_specs=(block, block, block, row, row, row),
        out_specs=block,
        check_vma=False,
    )
```

time: 856 us -> 135 us (0.16)
  the two profiles are of different devices: /device:TPU:9 before, /device:TPU:0 now
where the time goes in v1:
time: 135 us; the launch traced here: 134 us
  Pallas kernels  126 us (93%)
  local copies, waits for them, and re-layouts  4.44 us (3%)
  other arithmetic  3.66 us (3%)
    pallas_call x1, Pallas kernels, on_device(): pl.pallas_call(functools.partial(kernel, n, cap, sectors_l, channels), ou...  126 us
    unnamed x2, local copies, waits for them, and re-layouts  2.83 us

profile of v1, /device:TPU:0, one launch (start us, length us, event | category | flops | bytes accessed | tf_op | source)
XLA Modules:
  0.0 134.4 jit_solution(5476034935979275243)
XLA Ops:
  0.0 0.7 sign_compare_fusion
  0.7 0.1 ne.74
  0.8 0.8 add_bitcast_fusion
  1.5 0.7 select_reduce_fusion.3.place_ref
  2.2 0.7 broadcast_remainder_fusion
  2.9 0.1 rem.43
  3.0 0.1 div.29
  3.0 0.2 convert_reduce_fusion
  3.2 0.7 select_reduce_fusion
  3.9 0.1 reshape.96
  4.0 0.6 pad.4.request_ref
  4.6 0.8 copy.12
  5.4 0.7 reshape.97.pairs_ref
  6.1 126.3 %shard_map.64 = f32[12,128,128]{2,1,0:T(8,128)} custom-call(s32[16,1,128]{2,1,0:T(1,128)} %pad.4.request_ref, s32[128]{0:T(128)} %get-tuple-element.6.entry_ref, s32[128]{0:T(128)} %get-tuple-element.5.side_ref, s32[12]{0:T(128)} %select_reduce_fusion.3.place_ref, s32[24]{0:T(128)} %reshape.97.pairs_ref, s32[12,40]{1,0:T(8,128)} %mask_ref.1, ...), custom_call_target="tpu_custom_call" | custom-call | tf_op jit(solution)/shard_map/pallas_call | solution.py:226
  132.4 2.1 %copy.14 = f32[12,128,128]{2,1,0:T(8,128)} copy(f32[12,128,128]{2,1,0:T(8,128)} %shard_map.64) | data formatting | bytes 1572864
  (2 shorter events, 0.0 us)

commit v2 on v1

--- a/solution.py
+++ b/solution.py
@@ -22,12 +22,7 @@
 def kernel(
     n,
     cap,
-    sectors_l,
-    channels,
-    request_ref,
-    entry_ref,
-    side_ref,
-    place_ref,
+    env_ref,
     pairs_ref,
     mask_ref,
     psi_ref,
@@ -36,6 +31,8 @@
     out_ref,
     left,
     right,
+    table,
+    table_sc,
     asked,
     asked_sc,
     send,
@@ -53,6 +50,14 @@
     me = lax.axis_index("blk")
     tile = psi_ref.shape[1]
     pairs = psi_ref.shape[0]
+    channels = mask_ref.shape[1]
+    sectors_l = total.shape[0]
+    stored = right.shape[0]
+    lanes = asked.shape[2]
+
+    def step(i):
+        return n // 2 + (1 - 2 * (i % 2)) * ((i + 1) // 2)
+
     right_copy = pltpu.make_async_copy(right_hbm, right, right_sem)
     right_copy.start()
 
@@ -73,25 +78,49 @@
         return c
 
     lax.fori_loop(1, n, greet, 0)
+
+    used = env_ref.shape[0] * channels
+    height = -(-used // 128) * 128
+    sides = [env_ref[r : r + 1, :] for r in range(env_ref.shape[0])]
+    if height > used:
+        sides.append(jnp.full((1, height - used), n * stored, jnp.int32))
+    across = jnp.broadcast_to(jnp.concatenate(sides, axis=1), (height, height))
+    down = across.T
+    first = lax.broadcasted_iota(jnp.int32, (height, height), 0)
+    second = lax.broadcasted_iota(jnp.int32, (height, height), 1)
+    owner = lax.div(down, jnp.full_like(down, stored))
+    same = (owner == lax.div(across, jnp.full_like(across, stored))) & (second < first)
+    rank = jnp.sum(same.astype(jnp.int32), axis=1, keepdims=True)
+    slot = owner[:, :1] * cap + rank
+    entry = lax.broadcasted_iota(jnp.int32, (height, lanes), 0)
+    chosen = slot == lax.broadcasted_iota(jnp.int32, (height, lanes), 1)
+    local = down[:, :1] - owner[:, :1] * stored
+
+    def picked(values):
+        return jnp.sum(jnp.where(chosen, values, 0), axis=0, keepdims=True)
+
+    asked[0] = picked(jnp.broadcast_to(local, (height, lanes)))
+    table[0:1, :] = picked(entry)
+    table[1:2, :] = picked(1 + (entry >= channels).astype(jnp.int32))
+    table_copy = pltpu.make_async_copy(table, table_sc, table_sem.at[0])
+    table_copy.start()
     pl.semaphore_wait(barrier, n - 1)
 
     def ask(k):
-        peer = flip(me, k, n)
         return pltpu.make_async_remote_copy(
-            src_ref=request_ref.at[peer],
+            src_ref=asked.at[0],
             dst_ref=asked.at[k],
             send_sem=ask_send_sem.at[k],
             recv_sem=ask_recv_sem.at[k],
-            device_id={"blk": peer},
+            device_id={"blk": flip(me, k, n)},
             device_id_type=MESH,
         )
 
-    def ask_start(k, c):
-        ask(n - k).start()
-        return c
-
-    lax.fori_loop(1, n, ask_start, 0)
-    asked[0] = request_ref[me]
+    def ask_start(i, c):
+        ask(step(i)).start()
+        return c
+
+    lax.fori_loop(0, n - 1, ask_start, 0)
 
     def reply(k):
         return pltpu.make_async_remote_copy(
@@ -103,32 +132,35 @@
             device_id_type=MESH,
         )
 
-    def ask_wait(k, c):
-        ask(n - k).wait()
-        return c
-
-    lax.fori_loop(1, n, ask_wait, 0)
-    table_copy = pltpu.make_async_copy(asked, asked_sc, table_sem)
-    table_copy.start()
+    def ask_wait(i, c):
+        ask(step(i)).wait()
+        return c
+
+    lax.fori_loop(0, n - 1, ask_wait, 0)
+    asked_copy = pltpu.make_async_copy(asked, asked_sc, table_sem.at[1])
+    asked_copy.start()
     right_copy.wait()
-    table_copy.wait()
+    asked_copy.wait()
 
     def pack(i, c):
-        k = n - i
-
+        k = step(i)
         for j in range(cap):
-            send[k, j] = right[asked_sc[k, 0, j]]
+            send[k, j] = right[asked_sc[k, 0, me * cap + j]]
         reply(k).start()
         return c
 
-    lax.fori_loop(1, n, pack, 0)
+    lax.fori_loop(0, n - 1, pack, 0)
     for j in range(cap):
-        held[0, j] = right[asked_sc[0, 0, j]]
+        held[0, j] = right[asked_sc[0, 0, me * cap + j]]
 
     def lift(l, c):
         left_copy(l).wait()
-        p0 = place_ref[2 * l]
-        p1 = place_ref[2 * l + 1]
+        p0 = 0
+        p1 = 0
+        for p in range(pairs):
+            spot = 2 * pairs_ref[p, 0] + pairs_ref[p, 1]
+            p0 = jnp.where(spot == 2 * l, p, p0)
+            p1 = jnp.where(spot == 2 * l + 1, p, p1)
         state = jnp.concatenate([psi_ref[p0], psi_ref[p1]], axis=1)
 
         def one(a, c):
@@ -143,6 +175,7 @@
 
     lax.fori_loop(0, sectors_l, lift, 0)
     total[...] = jnp.zeros_like(total)
+    table_copy.wait()
 
     def apply(k):
         peer = flip(me, k, n)
@@ -152,10 +185,10 @@
             entries = []
             for j in range(2):
                 s = peer * cap + 2 * h + j
-                entries.append(entry_ref[s])
+                entries.append(table_sc[0, s])
                 block = held[k, 2 * h + j].astype(jnp.float32)
-                w0 = (side_ref[s] % 2).astype(jnp.float32)
-                w1 = (side_ref[s] // 2).astype(jnp.float32)
+                w0 = (table_sc[1, s] % 2).astype(jnp.float32)
+                w1 = (table_sc[1, s] // 2).astype(jnp.float32)
                 rows.append(
                     jnp.concatenate([(block * w0).astype(jnp.bfloat16), (block * w1).astype(jnp.bfloat16)], axis=0)
                 )
@@ -173,16 +206,16 @@
     apply(0)
 
     def arrive(i, c):
-        k = n - i
+        k = step(i)
         reply(k).wait_recv()
         apply(k)
         return c
 
-    lax.fori_loop(1, n, arrive, 0)
+    lax.fori_loop(0, n - 1, arrive, 0)
 
     def finish(p, c):
-        both = total[pairs_ref[2 * p]]
-        w1 = pairs_ref[2 * p + 1].astype(jnp.float32)
+        both = total[pairs_ref[p, 0]]
+        w1 = pairs_ref[p, 1].astype(jnp.float32)
         out_ref[p] = both[:, :tile] * (1.0 - w1) + both[:, tile:] * w1
         return c
 
@@ -205,34 +238,22 @@
     cap = max(2, (3 * used + 2 * n - 1) // (2 * n))
     cap += cap % 2
 
-    ids = right_env.reshape(used)
-    owners = ids // stored
-    order = jnp.arange(used, dtype=jnp.int32)
-    same = (owners[:, None] == owners[None, :]) & (order[None, :] < order[:, None])
-    rank = jnp.sum(same.astype(jnp.int32), axis=1)
-    slot = owners * cap + rank
-    chosen = slot[None, :] == jnp.arange(n * cap, dtype=jnp.int32)[:, None]
-    entry = jnp.sum(jnp.where(chosen, order[None, :], 0), axis=1)
-    side = jnp.sum(jnp.where(chosen, 1 + (order // channels)[None, :], 0), axis=1)
-    request = jnp.sum(jnp.where(chosen, (ids % stored)[None, :], 0), axis=1)
-    request = jnp.pad(request.reshape(n, 1, cap), ((0, 0), (0, 0), (0, 128 - cap)))
-    spot = pair_sectors[:, 0] * sides + pair_sectors[:, 1]
-    which = jnp.arange(pairs, dtype=jnp.int32)
-    place = jnp.sum(jnp.where(spot[None, :] == which[:, None], which[None, :], 0), axis=1)
-
+    lanes = -(-n * cap // 128) * 128
     smem = pl.BlockSpec(memory_space=pltpu.SMEM)
     vmem = pl.BlockSpec(memory_space=pltpu.VMEM)
     hbm = pl.BlockSpec(memory_space=pl.ANY)
     return pl.pallas_call(
-        functools.partial(kernel, n, cap, sectors_l, channels),
+        functools.partial(kernel, n, cap),
         out_shape=jax.ShapeDtypeStruct((pairs, tile, tile), jnp.float32),
-        in_specs=[vmem, smem, smem, smem, smem, smem, vmem, hbm, hbm],
+        in_specs=[vmem, smem, smem, vmem, hbm, hbm],
         out_specs=vmem,
         scratch_shapes=[
             pltpu.VMEM(left_blocks.shape, jnp.bfloat16),
             pltpu.VMEM(right_blocks.shape, jnp.bfloat16),
-            pltpu.VMEM((n, 1, 128), jnp.int32),
-            pltpu.SMEM((n, 1, 128), jnp.int32),
+            pltpu.VMEM((2, lanes), jnp.int32),
+            pltpu.SMEM((2, lanes), jnp.int32),
+            pltpu.VMEM((n, 1, lanes), jnp.int32),
+            pltpu.SMEM((n, 1, lanes), jnp.int32),
             pltpu.VMEM((n, cap, tile, tile), jnp.bfloat16),
             pltpu.VMEM((n, cap, tile, tile), jnp.bfloat16),
             pltpu.VMEM((used, sectors_l, tile, tile), jnp.bfloat16),
@@ -241,7 +262,7 @@
             pltpu.SemaphoreType.DMA,
             pltpu.SemaphoreType.DMA((n,)),
             pltpu.SemaphoreType.DMA((n,)),
-            pltpu.SemaphoreType.DMA,
+            pltpu.SemaphoreType.DMA((2,)),
             pltpu.SemaphoreType.DMA((n,)),
             pltpu.SemaphoreType.DMA((n,)),
         ],
@@ -249,11 +270,8 @@
             collective_id=0, has_side_effects=True, vmem_limit_bytes=56 * 1024 * 1024
         ),
     )(
-        request,
-        entry,
-        side,
-        place,
-        pair_sectors.reshape(-1),
+        right_env,
+        pair_sectors,
         channel_mask,
         wavefunction,
         left_blocks,

time: 135 us -> 109 us (0.81)
  the two profiles are of different devices: /device:TPU:0 before, /device:TPU:9 now
where the time goes in v2:
time: 109 us
  Pallas kernels  106 us (97%)
  local copies, waits for them, and re-layouts  3.42 us (3%)
    pallas_call x1, Pallas kernels, on_device(): pl.pallas_call(functools.partial(kernel, n, cap), out_shape=jax.ShapeDtyp...  106 us
    unnamed x2, local copies, waits for them, and re-layouts  3.42 us

profile of v2, /device:TPU:9, one launch (start us, length us, event | category | flops | bytes accessed | tf_op | source)
XLA Modules:
  0.0 109.0 jit_solution(3317783211842276924)
XLA Ops:
  0.0 1.4 %copy.7.pairs_ref = s32[12,2]{1,0:T(8,128)} copy(s32[12,2]{0,1:T(2,128)} %param.10) | data formatting | bytes 192 | tf_op args[4]
  1.4 105.5 %shard_map.64 = f32[12,128,128]{2,1,0:T(8,128)} custom-call(s32[2,40]{1,0:T(2,128)} %env_ref.1, s32[12,2]{1,0:T(8,128)} %copy.7.pairs_ref, s32[12,40]{1,0:T(8,128)} %mask_ref.1, bf16[12,128,128]{2,1,0:T(8,128)(2,1)} %psi_ref.1, bf16[240,128,128]{2,1,0:T(8,128)(2,1)} %left_hbm.1, bf16[80,128,128]{2,1,0:T(8,128)(2,1)} %right_hbm.1), custom_call_target="tpu_custom_call" | custom-call | tf_op jit(solution)/shard_map/pallas_call | solution.py:245
  106.9 2.1 %copy.9 = f32[12,128,128]{2,1,0:T(8,128)} copy(f32[12,128,128]{2,1,0:T(8,128)} %shard_map.64) | data formatting | bytes 1572864

commit v3 on v2

--- a/solution.py
+++ b/solution.py
@@ -54,6 +54,15 @@
     sectors_l = total.shape[0]
     stored = right.shape[0]
     lanes = asked.shape[2]
+    bits = [1 << b for b in range(n.bit_length() - 1)]
+    turn = [bit - 2 * bit * ((me // bit) % 2) for bit in bits]
+
+    def partner(k):
+        out = me
+        for bit, change in zip(bits, turn):
+            if k & bit:
+                out = out + change
+        return out
 
     def step(i):
         return n // 2 + (1 - 2 * (i % 2)) * ((i + 1) // 2)
@@ -68,33 +77,28 @@
             left_sem.at[l],
         )
 
-    for l in range(sectors_l):
-        left_copy(l).start()
-
     barrier = pltpu.get_barrier_semaphore()
 
-    def greet(k, c):
-        pl.semaphore_signal(barrier, inc=1, device_id={"blk": flip(me, k, n)}, device_id_type=MESH)
-        return c
-
-    lax.fori_loop(1, n, greet, 0)
+    for i in range(n - 1):
+        pl.semaphore_signal(barrier, inc=1, device_id={"blk": partner(step(i))}, device_id_type=MESH)
 
     used = env_ref.shape[0] * channels
     height = -(-used // 128) * 128
     sides = [env_ref[r : r + 1, :] for r in range(env_ref.shape[0])]
     if height > used:
         sides.append(jnp.full((1, height - used), n * stored, jnp.int32))
-    across = jnp.broadcast_to(jnp.concatenate(sides, axis=1), (height, height))
-    down = across.T
+    ids = jnp.concatenate(sides, axis=1)
+    owners = lax.div(ids, jnp.full_like(ids, stored))
+    across = jnp.broadcast_to(owners, (height, height))
+    owner = across.T
+    local = jnp.broadcast_to(ids - owners * stored, (height, height)).T[:, :1]
     first = lax.broadcasted_iota(jnp.int32, (height, height), 0)
     second = lax.broadcasted_iota(jnp.int32, (height, height), 1)
-    owner = lax.div(down, jnp.full_like(down, stored))
-    same = (owner == lax.div(across, jnp.full_like(across, stored))) & (second < first)
+    same = (owner == across) & (second < first)
     rank = jnp.sum(same.astype(jnp.int32), axis=1, keepdims=True)
     slot = owner[:, :1] * cap + rank
     entry = lax.broadcasted_iota(jnp.int32, (height, lanes), 0)
     chosen = slot == lax.broadcasted_iota(jnp.int32, (height, lanes), 1)
-    local = down[:, :1] - owner[:, :1] * stored
 
     def picked(values):
         return jnp.sum(jnp.where(chosen, values, 0), axis=0, keepdims=True)
@@ -112,44 +116,51 @@
             dst_ref=asked.at[k],
             send_sem=ask_send_sem.at[k],
             recv_sem=ask_recv_sem.at[k],
-            device_id={"blk": flip(me, k, n)},
+            device_id={"blk": partner(k)},
             device_id_type=MESH,
         )
 
-    def ask_start(i, c):
+    for i in range(n - 1):
         ask(step(i)).start()
-        return c
-
-    lax.fori_loop(0, n - 1, ask_start, 0)
-
-    def reply(k):
+
+    def reply(k, peer):
         return pltpu.make_async_remote_copy(
             src_ref=send.at[k],
             dst_ref=held.at[k],
             send_sem=send_sem.at[k],
             recv_sem=recv_sem.at[k],
-            device_id={"blk": flip(me, k, n)},
+            device_id={"blk": peer},
             device_id_type=MESH,
         )
 
-    def ask_wait(i, c):
-        ask(step(i)).wait()
-        return c
-
-    lax.fori_loop(0, n - 1, ask_wait, 0)
-    asked_copy = pltpu.make_async_copy(asked, asked_sc, table_sem.at[1])
-    asked_copy.start()
+    early = min(3, n - 1)
+
+    def serve(steps, spans):
+        for i in steps:
+            ask(step(i)).wait()
+        copies = [
+            pltpu.make_async_copy(asked.at[pl.ds(a, b - a)], asked_sc.at[pl.ds(a, b - a)], table_sem.at[1 + a])
+            for a, b in spans
+            if b > a
+        ]
+        for copy in copies:
+            copy.start()
+        for copy in copies:
+            copy.wait()
+        for i in steps:
+            k = step(i)
+            for j in range(cap):
+                send[k, j] = right[asked_sc[k, 0, me * cap + j]]
+            reply(k, partner(k)).start()
+
+    low = min(step(i) for i in range(early))
+    high = max(step(i) for i in range(early)) + 1
     right_copy.wait()
-    asked_copy.wait()
-
-    def pack(i, c):
-        k = step(i)
-        for j in range(cap):
-            send[k, j] = right[asked_sc[k, 0, me * cap + j]]
-        reply(k).start()
-        return c
-
-    lax.fori_loop(0, n - 1, pack, 0)
+    serve(range(early), [(low, high)])
+    serve(range(early, n - 1), [(0, low), (high, n)])
+    for l in range(sectors_l):
+        left_copy(l).start()
+
     for j in range(cap):
         held[0, j] = right[asked_sc[0, 0, me * cap + j]]
 
@@ -158,7 +169,7 @@
         p0 = 0
         p1 = 0
         for p in range(pairs):
-            spot = 2 * pairs_ref[p, 0] + pairs_ref[p, 1]
+            spot = 2 * pairs_ref[0, p] + pairs_ref[1, p]
             p0 = jnp.where(spot == 2 * l, p, p0)
             p1 = jnp.where(spot == 2 * l + 1, p, p1)
         state = jnp.concatenate([psi_ref[p0], psi_ref[p1]], axis=1)
@@ -207,25 +218,22 @@
 
     def arrive(i, c):
         k = step(i)
-        reply(k).wait_recv()
+        reply(k, flip(me, k, n)).wait_recv()
         apply(k)
         return c
 
     lax.fori_loop(0, n - 1, arrive, 0)
 
     def finish(p, c):
-        both = total[pairs_ref[p, 0]]
-        w1 = pairs_ref[p, 1].astype(jnp.float32)
+        both = total[pairs_ref[0, p]]
+        w1 = pairs_ref[1, p].astype(jnp.float32)
         out_ref[p] = both[:, :tile] * (1.0 - w1) + both[:, tile:] * w1
         return c
 
     lax.fori_loop(0, pairs, finish, 0)
 
-    def sent(k, c):
-        reply(k).wait_send()
-        return c
-
-    lax.fori_loop(1, n, sent, 0)
+    for k in range(1, n):
+        reply(k, partner(k)).wait_send()
 
 
 def on_device(n, wavefunction, left_blocks, right_blocks, right_env, pair_sectors, channel_mask):
@@ -262,7 +270,7 @@
             pltpu.SemaphoreType.DMA,
             pltpu.SemaphoreType.DMA((n,)),
             pltpu.SemaphoreType.DMA((n,)),
-            pltpu.SemaphoreType.DMA((2,)),
+            pltpu.SemaphoreType.DMA((n + 1,)),
             pltpu.SemaphoreType.DMA((n,)),
             pltpu.SemaphoreType.DMA((n,)),
         ],
@@ -271,7 +279,7 @@
         ),
     )(
         right_env,
-        pair_sectors,
+        pair_sectors.T,
         channel_mask,
         wavefunction,
         left_blocks,

time: 109 us -> 106 us (0.972)
  Pallas kernels: 106 us -> 104 us
  local copies, waits for them, and re-layouts: 3.42 us -> 2.06 us
    pallas_call x1, Pallas kernels: 106 us -> 104 us  [on_device(): pl.pallas_call(functools.partial(kernel, n, cap), out_shape=jax.ShapeDtyp...]
    unnamed x2 -> x1, local copies, waits for them, and re-layouts: 3.42 us -> 2.06 us
where the time goes in v3:
time: 106 us
  Pallas kernels  104 us (98%)
  local copies, waits for them, and re-layouts  2.06 us (2%)
    pallas_call x1, Pallas kernels, on_device(): pl.pallas_call(functools.partial(kernel, n, cap), out_shape=jax.ShapeDtyp...  104 us

profile of v3, /device:TPU:9, one launch (start us, length us, event | category | flops | bytes accessed | tf_op | source)
XLA Modules:
  0.0 106.1 jit_solution(12445458864452756955)
XLA Ops:
  0.0 104.1 %shard_map.64 = f32[12,128,128]{2,1,0:T(8,128)} custom-call(s32[2,40]{1,0:T(2,128)} %env_ref.1, s32[2,12]{1,0:T(2,128)} %bitcast.1, s32[12,40]{1,0:T(8,128)} %mask_ref.1, bf16[12,128,128]{2,1,0:T(8,128)(2,1)} %psi_ref.1, bf16[240,128,128]{2,1,0:T(8,128)(2,1)} %left_hbm.1, bf16[80,128,128]{2,1,0:T(8,128)(2,1)} %right_hbm.1), custom_call_target="tpu_custom_call" | custom-call | tf_op jit(solution)/shard_map/pallas_call | solution.py:253
  104.1 2.1 %copy.8 = f32[12,128,128]{2,1,0:T(8,128)} copy(f32[12,128,128]{2,1,0:T(8,128)} %shard_map.64) | data formatting | bytes 1572864

commit v4 on v3

--- a/solution.py
+++ b/solution.py
@@ -252,7 +252,7 @@
     hbm = pl.BlockSpec(memory_space=pl.ANY)
     return pl.pallas_call(
         functools.partial(kernel, n, cap),
-        out_shape=jax.ShapeDtypeStruct((pairs, tile, tile), jnp.float32),
+        out_shape=pltpu.VMEM((pairs, tile, tile), jnp.float32),
         in_specs=[vmem, smem, smem, vmem, hbm, hbm],
         out_specs=vmem,
         scratch_shapes=[

time: 106 us -> 104 us (0.981)
  local copies, waits for them, and re-layouts: 2.06 us -> 0.88 us
    unnamed x1, local copies, waits for them, and re-layouts: 2.06 us -> 0.88 us
where the time goes in v4:
time: 104 us
  Pallas kernels  103 us (99%)
    pallas_call x1, Pallas kernels, on_device(): pl.pallas_call(functools.partial(kernel, n, cap), out_shape=pltpu.VMEM((p...  103 us

profile of v4, /device:TPU:9, one launch (start us, length us, event | category | flops | bytes accessed | tf_op | source)
XLA Modules:
  0.0 104.1 jit_solution(14447330075447697994)
XLA Ops:
  0.0 103.2 %shard_map.64 = f32[12,128,128]{2,1,0:T(8,128)S(1)} custom-call(s32[2,40]{1,0:T(2,128)} %env_ref.1, s32[2,12]{1,0:T(2,128)} %bitcast.1, s32[12,40]{1,0:T(8,128)} %mask_ref.1, bf16[12,128,128]{2,1,0:T(8,128)(2,1)} %psi_ref.1, bf16[240,128,128]{2,1,0:T(8,128)(2,1)} %left_hbm.1, bf16[80,128,128]{2,1,0:T(8,128)(2,1)} %right_hbm.1), custom_call_target="tpu_custom_call" | custom-call | tf_op jit(solution)/shard_map/pallas_call | solution.py:253
  103.2 0.9 copy.8
